TPU v7x, 32 devices: a whole 2x2x4 slice. The times are simulated.
32 devices in a mesh: dp: 16 (over z, y, x), cls: 2 (over core).
Axes of the slice: x: 2, y: 2, z: 4, core: 2. Of those that a mesh axis runs over, the one named last changes fastest.
Arguments:
- scores: bfloat16 [32768, 1024], P('dp', 'cls'), may hold values from -4 to 250
- labels: int32 [32768], P('dp'), may hold values from 0 to 1023
- node_ids: int32 [32768], P('dp'), may hold values from 0 to 3
- codes: int32 [32768, 512], P('dp', 'cls'), may hold values from 0 to 255
- sketch: float32 [1024, 8], P('cls'), may hold values from -4 to 4
Outputs:
- histogram: float32 [256, 4, 9, 512], P('dp', None, None, 'cls')
All inputs are finite; a program needn't handle non-finite values.
Results may differ from a plain program's by a relative error of at most 0.002.
Values may be sent and summed in bfloat16 or wider, within the bound.
A program may use at most 128 MiB of HBM per device.

v0:
```python
import math

import jax
import jax.numpy as jnp
from jax import lax
from jax.sharding import PartitionSpec as P

BINS = 256
NODES = 4
STATS = 9


def body(scores, labels, node_ids, codes, sketch):
    row_count, class_local = scores.shape
    feat_local = codes.shape[1]
    offset = lax.axis_index("cls") * class_local
    values = scores.astype(jnp.float32)
    is_label = (
        labels[:, None] == offset + jnp.arange(class_local, dtype=jnp.int32)[None, :]
    ).astype(jnp.float32)
    label_term = jnp.dot(is_label, sketch, precision=lax.Precision.HIGHEST)
    narrow_top = jnp.max(scores, axis=1)
    top = lax.pmax(narrow_top, "cls").astype(jnp.float32)
    expo = jnp.exp(values - top[:, None])
    total = jnp.sum(expo, axis=1)
    squares = jnp.sum(expo * expo, axis=1)
    sketched = jnp.dot(expo, sketch, precision=lax.Precision.HIGHEST)
    total, squares, sketched, label_sum = lax.psum((total, squares, sketched, label_term), "cls")
    grad = sketched / total[:, None] - label_sum
    hessian = 1.0 - squares / (total * total)
    stats = jnp.concatenate([grad, hessian[:, None]], axis=1)
    member = (node_ids[:, None] == jnp.arange(NODES, dtype=jnp.int32)[None, :]).astype(jnp.float32)
    weighted = (
        (member[:, :, None] * stats[:, None, :])
        .reshape(row_count, NODES * STATS)
        .astype(jnp.bfloat16)
    )
    group = NODES * STATS
    count = BINS * group
    first_bin = 0 // group
    bin_count = count // group
    block = max(math.gcd(bin_count, 16), 2)

    def one_block(step):
        lowest = first_bin + step * block
        targets = lowest + jnp.arange(block, dtype=jnp.int32)
        hits = (codes[:, None, :] == targets[None, :, None]).astype(jnp.bfloat16)
        hits = hits.reshape(row_count, block * feat_local)
        part = lax.dot_general(
            weighted, hits, (((0,), (0,)), ((), ())), preferred_element_type=jnp.float32
        )
        part = part.reshape(group, block, feat_local).transpose(1, 0, 2)
        return part.reshape(block * group, feat_local)

    blocks = lax.map(one_block, jnp.arange(bin_count // block, dtype=jnp.int32))
    flat = lax.psum_scatter(
        blocks.reshape(count, feat_local), "dp", scatter_dimension=0, tiled=True
    )
    return flat.reshape(-1, NODES, STATS, feat_local)


def solution(mesh):
    return jax.shard_map(
        body,
        mesh=mesh,
        in_specs=(P("dp", "cls"), P("dp"), P("dp"), P("dp", "cls"), P("cls", None)),
        out_specs=P("dp", None, None, "cls"),
        check_vma=False,
    )
```

profile of v0, /device:TPU:15, one launch (start us, length us, event | category | flops | bytes accessed | tf_op | source)
XLA Modules:
  0.0 1105.6 jit_solution(8507957490316231032)
XLA Ops:
  41.2 885.7 %while.11 = (s32[]{:T(128)}, f32[16,576,256]{2,1,0:T(8,128)}, s32[2048,256]{1,0:T(8,128)S(1)}, s32[16]{0:T(128)S(1)}, f32[2048,9]{0,1:T(8,128)S(1)}, /*index=5*/f32[2048,4]{0,1:T(4,128)S(1)}, s32[]{:T(128)}, s32[1]{0:T(128)}) while((s32[]{:T(128)}, f32[16,576,256]{2,1,0:T(8,128)}, s32[2048,256]{1,0:T(8,128)S(1)}, ...), condition=%wide.region_9.10_spmd.clone, body=%wide.region_8.9_spmd.clone.sunk | while | flops 612515840 | bytes 143696128 | solution.py:55
  44.1 36.2 %copy.20 = s32[256,8,16,256]{3,1,2,0:T(8,128)} copy(s32[256,8,16,256]{3,2,1,0:T(8,128)S(1)} %bitcast.39) | data formatting | bytes 67108864 | tf_op jit(solution)/shard_map/while
  81.7 13.3 %fusion.21 = f32[4096,36]{0,1:T(8,128)S(1)} fusion(bf16[2048,36]{0,1:T(8,128)(2,1)S(1)} %convert_element_type.45, s32[2048,4096]{1,0:T(8,128)} %bitcast.38, s32[4096]{0:T(1024)S(1)} %bitcast.44), kind=kOutput, calls=%fused_computation.1.clone.1 | convolution fusion | flops 612368384 | bytes 34308096 | tf_op jit(solution)/shard_map/while/body/eval_jaxpr/dot_general | solution.py:49
  99.5 36.2 %copy.20 = s32[256,8,16,256]{3,1,2,0:T(8,128)} copy(s32[256,8,16,256]{3,2,1,0:T(8,128)S(1)} %bitcast.39) | data formatting | bytes 67108864 | tf_op jit(solution)/shard_map/while
  154.8 36.2 %copy.20 = s32[256,8,16,256]{3,1,2,0:T(8,128)} copy(s32[256,8,16,256]{3,2,1,0:T(8,128)S(1)} %bitcast.39) | data formatting | bytes 67108864 | tf_op jit(solution)/shard_map/while
  192.4 13.3 %fusion.21 = f32[4096,36]{0,1:T(8,128)S(1)} fusion(bf16[2048,36]{0,1:T(8,128)(2,1)S(1)} %convert_element_type.45, s32[2048,4096]{1,0:T(8,128)} %bitcast.38, s32[4096]{0:T(1024)S(1)} %bitcast.44), kind=kOutput, calls=%fused_computation.1.clone.1 | convolution fusion | flops 612368384 | bytes 34308096 | tf_op jit(solution)/shard_map/while/body/eval_jaxpr/dot_general | solution.py:49
  210.2 36.2 %copy.20 = s32[256,8,16,256]{3,1,2,0:T(8,128)} copy(s32[256,8,16,256]{3,2,1,0:T(8,128)S(1)} %bitcast.39) | data formatting | bytes 67108864 | tf_op jit(solution)/shard_map/while
  247.8 13.3 %fusion.21 = f32[4096,36]{0,1:T(8,128)S(1)} fusion(bf16[2048,36]{0,1:T(8,128)(2,1)S(1)} %convert_element_type.45, s32[2048,4096]{1,0:T(8,128)} %bitcast.38, s32[4096]{0:T(1024)S(1)} %bitcast.44), kind=kOutput, calls=%fused_computation.1.clone.1 | convolution fusion | flops 612368384 | bytes 34308096 | tf_op jit(solution)/shard_map/while/body/eval_jaxpr/dot_general | solution.py:49
  265.5 36.2 %copy.20 = s32[256,8,16,256]{3,1,2,0:T(8,128)} copy(s32[256,8,16,256]{3,2,1,0:T(8,128)S(1)} %bitcast.39) | data formatting | bytes 67108864 | tf_op jit(solution)/shard_map/while
  303.1 13.3 %fusion.21 = f32[4096,36]{0,1:T(8,128)S(1)} fusion(bf16[2048,36]{0,1:T(8,128)(2,1)S(1)} %convert_element_type.45, s32[2048,4096]{1,0:T(8,128)} %bitcast.38, s32[4096]{0:T(1024)S(1)} %bitcast.44), kind=kOutput, calls=%fused_computation.1.clone.1 | convolution fusion | flops 612368384 | bytes 34308096 | tf_op jit(solution)/shard_map/while/body/eval_jaxpr/dot_general | solution.py:49
  320.9 36.2 %copy.20 = s32[256,8,16,256]{3,1,2,0:T(8,128)} copy(s32[256,8,16,256]{3,2,1,0:T(8,128)S(1)} %bitcast.39) | data formatting | bytes 67108864 | tf_op jit(solution)/shard_map/while
  358.5 13.3 %fusion.21 = f32[4096,36]{0,1:T(8,128)S(1)} fusion(bf16[2048,36]{0,1:T(8,128)(2,1)S(1)} %convert_element_type.45, s32[2048,4096]{1,0:T(8,128)} %bitcast.38, s32[4096]{0:T(1024)S(1)} %bitcast.44), kind=kOutput, calls=%fused_computation.1.clone.1 | convolution fusion | flops 612368384 | bytes 34308096 | tf_op jit(solution)/shard_map/while/body/eval_jaxpr/dot_general | solution.py:49
  376.3 36.2 %copy.20 = s32[256,8,16,256]{3,1,2,0:T(8,128)} copy(s32[256,8,16,256]{3,2,1,0:T(8,128)S(1)} %bitcast.39) | data formatting | bytes 67108864 | tf_op jit(solution)/shard_map/while
  413.8 13.3 %fusion.21 = f32[4096,36]{0,1:T(8,128)S(1)} fusion(bf16[2048,36]{0,1:T(8,128)(2,1)S(1)} %convert_element_type.45, s32[2048,4096]{1,0:T(8,128)} %bitcast.38, s32[4096]{0:T(1024)S(1)} %bitcast.44), kind=kOutput, calls=%fused_computation.1.clone.1 | convolution fusion | flops 612368384 | bytes 34308096 | tf_op jit(solution)/shard_map/while/body/eval_jaxpr/dot_general | solution.py:49
  431.6 36.2 %copy.20 = s32[256,8,16,256]{3,1,2,0:T(8,128)} copy(s32[256,8,16,256]{3,2,1,0:T(8,128)S(1)} %bitcast.39) | data formatting | bytes 67108864 | tf_op jit(solution)/shard_map/while
  469.2 13.3 %fusion.21 = f32[4096,36]{0,1:T(8,128)S(1)} fusion(bf16[2048,36]{0,1:T(8,128)(2,1)S(1)} %convert_element_type.45, s32[2048,4096]{1,0:T(8,128)} %bitcast.38, s32[4096]{0:T(1024)S(1)} %bitcast.44), kind=kOutput, calls=%fused_computation.1.clone.1 | convolution fusion | flops 612368384 | bytes 34308096 | tf_op jit(solution)/shard_map/while/body/eval_jaxpr/dot_general | solution.py:49
  487.0 36.2 %copy.20 = s32[256,8,16,256]{3,1,2,0:T(8,128)} copy(s32[256,8,16,256]{3,2,1,0:T(8,128)S(1)} %bitcast.39) | data formatting | bytes 67108864 | tf_op jit(solution)/shard_map/while
  524.5 13.3 %fusion.21 = f32[4096,36]{0,1:T(8,128)S(1)} fusion(bf16[2048,36]{0,1:T(8,128)(2,1)S(1)} %convert_element_type.45, s32[2048,4096]{1,0:T(8,128)} %bitcast.38, s32[4096]{0:T(1024)S(1)} %bitcast.44), kind=kOutput, calls=%fused_computation.1.clone.1 | convolution fusion | flops 612368384 | bytes 34308096 | tf_op jit(solution)/shard_map/while/body/eval_jaxpr/dot_general | solution.py:49
  542.3 36.2 %copy.20 = s32[256,8,16,256]{3,1,2,0:T(8,128)} copy(s32[256,8,16,256]{3,2,1,0:T(8,128)S(1)} %bitcast.39) | data formatting | bytes 67108864 | tf_op jit(solution)/shard_map/while
  579.9 13.3 %fusion.21 = f32[4096,36]{0,1:T(8,128)S(1)} fusion(bf16[2048,36]{0,1:T(8,128)(2,1)S(1)} %convert_element_type.45, s32[2048,4096]{1,0:T(8,128)} %bitcast.38, s32[4096]{0:T(1024)S(1)} %bitcast.44), kind=kOutput, calls=%fused_computation.1.clone.1 | convolution fusion | flops 612368384 | bytes 34308096 | tf_op jit(solution)/shard_map/while/body/eval_jaxpr/dot_general | solution.py:49
  597.7 36.2 %copy.20 = s32[256,8,16,256]{3,1,2,0:T(8,128)} copy(s32[256,8,16,256]{3,2,1,0:T(8,128)S(1)} %bitcast.39) | data formatting | bytes 67108864 | tf_op jit(solution)/shard_map/while
  635.2 13.3 %fusion.21 = f32[4096,36]{0,1:T(8,128)S(1)} fusion(bf16[2048,36]{0,1:T(8,128)(2,1)S(1)} %convert_element_type.45, s32[2048,4096]{1,0:T(8,128)} %bitcast.38, s32[4096]{0:T(1024)S(1)} %bitcast.44), kind=kOutput, calls=%fused_computation.1.clone.1 | convolution fusion | flops 612368384 | bytes 34308096 | tf_op jit(solution)/shard_map/while/body/eval_jaxpr/dot_general | solution.py:49
  653.0 36.2 %copy.20 = s32[256,8,16,256]{3,1,2,0:T(8,128)} copy(s32[256,8,16,256]{3,2,1,0:T(8,128)S(1)} %bitcast.39) | data formatting | bytes 67108864 | tf_op jit(solution)/shard_map/while
  690.6 13.3 %fusion.21 = f32[4096,36]{0,1:T(8,128)S(1)} fusion(bf16[2048,36]{0,1:T(8,128)(2,1)S(1)} %convert_element_type.45, s32[2048,4096]{1,0:T(8,128)} %bitcast.38, s32[4096]{0:T(1024)S(1)} %bitcast.44), kind=kOutput, calls=%fused_computation.1.clone.1 | convolution fusion | flops 612368384 | bytes 34308096 | tf_op jit(solution)/shard_map/while/body/eval_jaxpr/dot_general | solution.py:49
  708.4 36.2 %copy.20 = s32[256,8,16,256]{3,1,2,0:T(8,128)} copy(s32[256,8,16,256]{3,2,1,0:T(8,128)S(1)} %bitcast.39) | data formatting | bytes 67108864 | tf_op jit(solution)/shard_map/while
  763.7 36.2 %copy.20 = s32[256,8,16,256]{3,1,2,0:T(8,128)} copy(s32[256,8,16,256]{3,2,1,0:T(8,128)S(1)} %bitcast.39) | data formatting | bytes 67108864 | tf_op jit(solution)/shard_map/while
  801.3 13.3 %fusion.21 = f32[4096,36]{0,1:T(8,128)S(1)} fusion(bf16[2048,36]{0,1:T(8,128)(2,1)S(1)} %convert_element_type.45, s32[2048,4096]{1,0:T(8,128)} %bitcast.38, s32[4096]{0:T(1024)S(1)} %bitcast.44), kind=kOutput, calls=%fused_computation.1.clone.1 | convolution fusion | flops 612368384 | bytes 34308096 | tf_op jit(solution)/shard_map/while/body/eval_jaxpr/dot_general | solution.py:49
  819.1 36.2 %copy.20 = s32[256,8,16,256]{3,1,2,0:T(8,128)} copy(s32[256,8,16,256]{3,2,1,0:T(8,128)S(1)} %bitcast.39) | data formatting | bytes 67108864 | tf_op jit(solution)/shard_map/while
  856.6 13.3 %fusion.21 = f32[4096,36]{0,1:T(8,128)S(1)} fusion(bf16[2048,36]{0,1:T(8,128)(2,1)S(1)} %convert_element_type.45, s32[2048,4096]{1,0:T(8,128)} %bitcast.38, s32[4096]{0:T(1024)S(1)} %bitcast.44), kind=kOutput, calls=%fused_computation.1.clone.1 | convolution fusion | flops 612368384 | bytes 34308096 | tf_op jit(solution)/shard_map/while/body/eval_jaxpr/dot_general | solution.py:49
  874.4 36.2 %copy.20 = s32[256,8,16,256]{3,1,2,0:T(8,128)} copy(s32[256,8,16,256]{3,2,1,0:T(8,128)S(1)} %bitcast.39) | data formatting | bytes 67108864 | tf_op jit(solution)/shard_map/while
  912.0 13.3 %fusion.21 = f32[4096,36]{0,1:T(8,128)S(1)} fusion(bf16[2048,36]{0,1:T(8,128)(2,1)S(1)} %convert_element_type.45, s32[2048,4096]{1,0:T(8,128)} %bitcast.38, s32[4096]{0:T(1024)S(1)} %bitcast.44), kind=kOutput, calls=%fused_computation.1.clone.1 | convolution fusion | flops 612368384 | bytes 34308096 | tf_op jit(solution)/shard_map/while/body/eval_jaxpr/dot_general | solution.py:49
  926.9 169.4 %reduce-scatter.2.cloned.1.call-done = f32[576,256]{1,0:T(8,128)} async-done(((f32[9216,256]{1,0:T(8,128)}), f32[576,256]{1,0:T(8,128)}) %reduce-scatter.2.cloned.1.call-update) | async-done | bytes 589840 | tf_op jit(solution)/shard_map/reduce_scatter | solution.py:56
  (225 shorter events, 145.0 us)
Async XLA Ops:
  6.5 5.0 copy-start
  6.5 11.3 %copy-start.4 = (s32[2048]{0:T(1024)S(1)}, s32[2048]{0:T(1024)}, u32[]{:S(2)}) copy-start(s32[2048]{0:T(1024)} %param.8) | copy-start | bytes 24580
  6.5 33.7 %all-reduce.4.cloned.1.call-start = ((), (), s32[]{:S(2)}) async-start(), calls=%async_computation.2 | async-start | bytes 262144 | tf_op jit(solution)/shard_map/psum | solution.py:28
  6.5 17.0 %copy-start.3 = (s32[2048]{0:T(1024)S(1)}, s32[2048]{0:T(1024)}, u32[]{:S(2)}) copy-start(s32[2048]{0:T(1024)} %param.9) | copy-start | bytes 24580
  6.5 34.6 %copy-start.2 = (s32[2048,256]{1,0:T(8,128)S(1)}, s32[2048,256]{1,0:T(8,128)}, u32[]{:S(2)}) copy-start(s32[2048,256]{1,0:T(8,128)} %param.10) | copy-start | bytes 6291460
  20.6 1075.7 %reduce-scatter.2.cloned.1.call-start = ((), (), s32[]{:S(2)}) async-start(), calls=%async_computation.1 | async-start | bytes 10027008 | tf_op jit(solution)/shard_map/reduce_scatter | solution.py:56
  926.9 171.8 %copy-start.1 = (f32[512,8]{0,1:T(8,128)S(1)}, f32[512,8]{0,1:T(8,128)}, u32[]{:S(2)}) copy-start(f32[512,8]{0,1:T(8,128)} %param.11) | copy-start | bytes 49156
Sparse Core Ops, SparseCore 0:
  20.7 19.4 all-reduce.3
  927.0 169.2 reduce-scatter.1
where the time goes:
time: 1110 us
  local copies, waits for them, and re-layouts  663 us (60%)
  matrix products  222 us (20%)
  waiting for transfers between devices  183 us (16%)
  between operations  13.5 us (1%)
  loops' own time  11.5 us (1%)
    while x64, local copies, waits for them, and re-layouts  584 us
    dot_general x16, matrix products, one_block(): lax.dot_general(weighted, hits, (((0,), (0,)), ((), ())), preferred_eleme...  213 us
    reduce_scatter x1, waiting for transfers between devices, body(): lax.psum_scatter(blocks.reshape(count, feat_local), 'dp', scatter_dimensi...  169 us
    eq x16, local copies, waits for them, and re-layouts, one_block(): hits = (codes[:, None, :] == targets[None, :, None]).astype(jnp.bfloat16)  44.7 us
  transfers between devices with their start and end apart: 2, of which 2 were waited for; matrix products, arithmetic and copies ran while one was open for 0% of the time, Pallas kernels for 0%

commit v1 on v0

v1 whole, which is shorter than its diff:
```python
import functools

import jax
import jax.numpy as jnp
from jax import lax
from jax.experimental import pallas as pl
from jax.experimental.pallas import tpu as pltpu
from jax.sharding import PartitionSpec as P

BINS = 256
NODES = 4
STATS = 9
SLOT = 16
HIGH = lax.Precision.HIGHEST
NT = (((1,), (1,)), ((), ()))


def codes_kernel(codes_ref, out_ref):
    out_ref[...] = codes_ref[...].astype(jnp.float32).T.astype(jnp.bfloat16)


def softmax_kernel(scores_ref, labels_ref, sketch_ref, out_ref):
    values = scores_ref[...].astype(jnp.float32)
    rows, classes = values.shape
    top = jnp.max(values, axis=1, keepdims=True)
    expo = jnp.exp(values - top)
    left = sketch_ref[...]
    sums = lax.dot_general(left, expo, NT, precision=HIGH, preferred_element_type=jnp.float32)
    squares = lax.dot_general(
        left[8:16], expo * expo, NT, precision=HIGH, preferred_element_type=jnp.float32
    )
    hit = lax.broadcasted_iota(jnp.int32, (classes, rows), 0) == labels_ref[...]
    picked = jnp.dot(
        left[0:8], hit.astype(jnp.float32), precision=HIGH, preferred_element_type=jnp.float32
    )
    tops = jnp.broadcast_to(top, (rows, 128)).T[0:1]
    out_ref[0:8] = sums[0:8]
    out_ref[8:16] = picked
    where = lax.broadcasted_iota(jnp.int32, (8, rows), 0)
    out_ref[16:24] = jnp.where(where == 0, tops, jnp.where(where == 1, sums[8:9], squares[0:1]))


def stats_kernel(parts_ref, nodes_ref, out_ref):
    parts = parts_ref.shape[0]
    top = parts_ref[0, 16:17]
    for i in range(1, parts):
        top = jnp.maximum(top, parts_ref[i, 16:17])
    sketched = label = total = squares = 0.0
    for i in range(parts):
        scale = jnp.exp(parts_ref[i, 16:17] - top)
        sketched += parts_ref[i, 0:8] * scale
        label += parts_ref[i, 8:16]
        total += parts_ref[i, 17:18] * scale
        squares += parts_ref[i, 18:19] * (scale * scale)
    grad = sketched / total - label
    hessian = 1.0 - squares / (total * total)
    where = lax.broadcasted_iota(jnp.int32, grad.shape, 0)
    tail = jnp.where(where == 0, hessian, jnp.where(where == 1, nodes_ref[...].astype(jnp.float32), 0.0))
    out_ref[...] = jnp.concatenate([grad, tail], axis=0).astype(jnp.bfloat16)


def hist_kernel(pair, width, codes_ref, stats_ref, out_ref, left_ref, acc_ref):
    step = pl.program_id(0)
    rows = stats_ref.shape[2]
    feats = codes_ref.shape[1]
    groups = feats // pair

    @pl.when(step == 0)
    def _():
        acc_ref[...] = jnp.zeros_like(acc_ref)

    stats = stats_ref[0]
    node = stats[STATS:STATS + 1].astype(jnp.float32)
    wide = stats.astype(jnp.float32)
    wide = jnp.where(lax.broadcasted_iota(jnp.int32, wide.shape, 0) < STATS, wide, 0.0)
    blank = jnp.zeros((NODES * SLOT, rows), jnp.bfloat16)
    member = jnp.concatenate(
        [jnp.where(node == n, wide, 0.0).astype(jnp.bfloat16) for n in range(NODES)], axis=0
    )
    for i in range(pair):
        left_ref[i] = jnp.concatenate([member if i == k else blank for k in range(2)], axis=0)

    bins = lax.broadcasted_iota(jnp.int32, (BINS, width), 0).astype(jnp.bfloat16)
    one = jnp.ones((), jnp.bfloat16)
    zero = jnp.zeros((), jnp.bfloat16)
    for g in range(groups):
        total = acc_ref[g]
        for i in range(pair):
            for c in range(rows // width):
                cut = slice(c * width, (c + 1) * width)
                row = i * groups + g
                code = codes_ref[0, row:row + 1, cut]
                hit = jnp.where(code == bins, one, zero)
                total += lax.dot_general(
                    hit, left_ref[i, :, cut], NT, preferred_element_type=jnp.float32
                )
        acc_ref[g] = total

    @pl.when(step == pl.num_programs(0) - 1)
    def _():
        for g in range(groups):
            out_ref[:, g, :] = acc_ref[g]


def place_kernel(pair, in_ref, out_ref):
    devices, _, groups, lanes = in_ref.shape
    span = devices * groups
    block = in_ref[:, 0].reshape(span, lanes).T
    for i in range(pair):
        for n in range(NODES):
            at = (i * NODES + n) * SLOT
            out_ref[0, n, :, i * span:(i + 1) * span] = block[at:at + STATS]


def body(dp, scores, labels, node_ids, codes, sketch):
    rows, classes = scores.shape
    feats = codes.shape[1]
    own = feats // dp
    pair = 2 if own % 2 == 0 else 1
    groups = own // pair
    block = min(512, rows)

    codes_t = pl.pallas_call(
        codes_kernel,
        grid=(rows // block,),
        in_specs=[pl.BlockSpec((block, feats), lambda i: (i, 0))],
        out_specs=pl.BlockSpec((feats, block), lambda i: (0, i)),
        out_shape=jax.ShapeDtypeStruct((feats, rows), jnp.bfloat16),
    )(codes)
    codes_t = codes_t.reshape(pair, dp, groups, rows).transpose(1, 0, 2, 3).reshape(dp, own, rows)
    codes_all = lax.all_to_all(codes_t, "dp", 0, 0, tiled=True)

    local = (labels - lax.axis_index("cls") * classes)[None, :]
    left = jnp.concatenate(
        [sketch.T, jnp.ones((1, classes), jnp.float32), jnp.zeros((7, classes), jnp.float32)], axis=0
    )
    parts = pl.pallas_call(
        softmax_kernel,
        grid=(rows // block,),
        in_specs=[
            pl.BlockSpec((block, classes), lambda i: (i, 0)),
            pl.BlockSpec((1, block), lambda i: (0, i)),
            pl.BlockSpec((16, classes), lambda i: (0, 0)),
        ],
        out_specs=pl.BlockSpec((24, block), lambda i: (0, i)),
        out_shape=jax.ShapeDtypeStruct((24, rows), jnp.float32),
    )(scores, local, left)
    parts = lax.all_gather(parts, "cls")
    stats = pl.pallas_call(
        stats_kernel,
        out_shape=jax.ShapeDtypeStruct((SLOT, rows), jnp.bfloat16),
    )(parts, node_ids[None, :])
    stats = lax.all_gather(stats, "dp")

    hist = pl.pallas_call(
        functools.partial(hist_kernel, pair, min(WIDTH, rows)),
        grid=(dp,),
        in_specs=[
            pl.BlockSpec((1, own, rows), lambda i: (i, 0, 0)),
            pl.BlockSpec((1, SLOT, rows), lambda i: (i, 0, 0)),
        ],
        out_specs=pl.BlockSpec((BINS, groups, 128), lambda i: (0, 0, 0)),
        out_shape=jax.ShapeDtypeStruct((BINS, groups, 128), jnp.float32),
        scratch_shapes=[
            pltpu.VMEM((pair, 128, rows), jnp.bfloat16),
            pltpu.VMEM((groups, BINS, 128), jnp.float32),
        ],
        compiler_params=pltpu.CompilerParams(vmem_limit_bytes=40 << 20),
    )(codes_all, stats)
    bins = BINS // dp
    hist = lax.all_to_all(hist.reshape(dp, bins, groups, 128), "dp", 0, 0, tiled=True)
    return pl.pallas_call(
        functools.partial(place_kernel, pair),
        grid=(bins,),
        in_specs=[pl.BlockSpec((dp, 1, groups, 128), lambda i: (0, i, 0, 0))],
        out_specs=pl.BlockSpec((1, NODES, STATS, feats), lambda i: (i, 0, 0, 0)),
        out_shape=jax.ShapeDtypeStruct((bins, NODES, STATS, feats), jnp.float32),
    )(hist)


WIDTH = 256


def solution(mesh):
    return jax.shard_map(
        functools.partial(body, mesh.shape["dp"]),
        mesh=mesh,
        in_specs=(P("dp", "cls"), P("dp"), P("dp"), P("dp", "cls"), P("cls", None)),
        out_specs=P("dp", None, None, "cls"),
        check_vma=False,
    )
```

time: 1110 us -> 219 us (0.20)
  the two profiles are of different devices: /device:TPU:15 before, /device:TPU:0 now
where the time goes in v1:
time: 219 us; the launch traced here: 218 us
  Pallas kernels  98.9 us (45%)
  waiting for transfers between devices  56.8 us (26%)
  blocking collectives  33.3 us (15%)
  between operations  13.4 us (6%)
  starting transfers between devices  8.35 us (4%)
  local copies, waits for them, and re-layouts  6.15 us (3%)
    pallas_call x1, Pallas kernels, body(): pl.pallas_call(functools.partial(hist_kernel, pair, min(WIDTH, rows)), gr...  72.2 us
    all_gather x1, waiting for transfers between devices, body(): stats = lax.all_gather(stats, 'dp')  50.9 us
    all_to_all x1, blocking collectives, body(): lax.all_to_all(hist.reshape(dp, bins, groups, 128), 'dp', 0, 0, tiled=True)  29.6 us
    pallas_call x1, Pallas kernels, body(): pl.pallas_call(softmax_kernel, grid=(rows // block,), in_specs=[pl.BlockS...  11.8 us
    pallas_call x1, Pallas kernels, body(): pl.pallas_call(functools.partial(place_kernel, pair), grid=(bins,), in_sp...  9.36 us
    all_to_all x1, starting transfers between devices, body(): codes_all = lax.all_to_all(codes_t, 'dp', 0, 0, tiled=True)  8.31 us
    all_to_all x1, waiting for transfers between devices, body(): codes_all = lax.all_to_all(codes_t, 'dp', 0, 0, tiled=True)  5.82 us
  transfers between devices with their start and end apart: 2, of which 2 were waited for; matrix products, arithmetic and copies ran while one was open for 1% of the time, Pallas kernels for 6%

profile of v1, /device:TPU:0, one launch (start us, length us, event | category | flops | bytes accessed | tf_op | source)
XLA Modules:
  0.0 218.1 jit_solution(14160458333577791795)
XLA Ops:
  6.5 3.9 %shard_map.55 = bf16[256,2048]{1,0:T(8,128)(2,1)} custom-call(s32[2048,256]{1,0:T(8,128)} %codes_ref.1), custom_call_target="tpu_custom_call" | custom-call | tf_op jit(solution)/shard_map/pallas_call | solution.py:123
  10.4 0.0 copy-start.2
  10.4 0.0 copy-start.1
  10.4 2.3 %copy.9 = bf16[2,16,8,2048]{3,2,0,1:T(8,128)(2,1)} copy(bf16[2,16,8,2048]{3,2,1,0:T(8,128)(2,1)} %bitcast.15) | data formatting | bytes 2097152 | tf_op jit(solution)/shard_map/reshape | solution.py:130
  12.7 8.3 %all-to-all-start = ((bf16[16,16,2048]{2,1,0:T(8,128)(2,1)}), bf16[16,16,2048]{2,1,0:T(8,128)(2,1)S(1)}, u32[]{:S(2)}, u32[]{:S(2)}) async-start(bf16[16,16,2048]{2,1,0:T(8,128)(2,1)} %bitcast.12), calls=%async_computation | async-start | bytes 2097152 | tf_op jit(solution)/shard_map/all_to_all | solution.py:131
  21.1 0.0 all-gather.4.cloned.1.call-start
  21.1 0.1 pad.2.clone
  21.2 0.1 pad.1.clone
  21.3 0.0 copy-done.2
  21.3 0.6 broadcast_subtract_fusion
  21.9 0.0 copy-done.1
  21.9 0.7 maximum_maximum_fusion.sketch_ref
  22.6 11.8 %shard_map.56 = f32[24,2048]{1,0:T(8,128)} custom-call(bf16[2048,512]{1,0:T(8,128)(2,1)} %scores_ref.1, s32[1,2048]{1,0:T(1,128)} %bitcast.17, f32[16,512]{1,0:T(8,128)} %maximum_maximum_fusion.sketch_ref), custom_call_target="tpu_custom_call" | custom-call | tf_op jit(solution)/shard_map/pallas_call | solution.py:137
  34.3 3.7 %all-gather = f32[48,2048]{1,0:T(8,128)} all-gather(f32[24,2048]{1,0:T(8,128)} %shard_map.56), channel_id=2, replica_groups=mesh['dp'=16,'cls'=2] {'cls'}, dimensions={0}, use_global_device_ids=true | all-gather | bytes 589824 | tf_op jit(solution)/shard_map/all_gather | solution.py:148
  38.0 1.7 shard_map.57
  39.7 0.0 all-gather.4.cloned.1.call-update
  39.7 5.8 %all-to-all-done.codes_ref = bf16[16,16,2048]{2,1,0:T(8,128)(2,1)S(1)} async-done(((bf16[16,16,2048]{2,1,0:T(8,128)(2,1)}), bf16[16,16,2048]{2,1,0:T(8,128)(2,1)S(1)}, u32[]{:S(2)}, u32[]{:S(2)}) %all-to-all-start) | async-done | bytes 1048608 | tf_op jit(solution)/shard_map/all_to_all | solution.py:131
  45.5 50.9 %all-gather.4.cloned.1.call-done = bf16[256,2048]{1,0:T(8,128)(2,1)} async-done(((bf16[16,2048]{1,0:T(8,128)(2,1)}), bf16[256,2048]{1,0:T(8,128)(2,1)}) %all-gather.4.cloned.1.call-update) | async-done | bytes 1048592 | tf_op jit(solution)/shard_map/all_gather | solution.py:153
  96.4 0.0 copy-start
  96.4 1.2 copy-done
  97.7 72.2 %shard_map.58 = f32[256,8,128]{2,1,0:T(8,128)S(1)} custom-call(bf16[16,16,2048]{2,1,0:T(8,128)(2,1)S(1)} %all-to-all-done.codes_ref, bf16[16,16,2048]{2,1,0:T(8,128)(2,1)S(1)} %bitcast.14), custom_call_target="tpu_custom_call" | custom-call | tf_op jit(solution)/shard_map/pallas_call | solution.py:155
  169.9 29.6 %all_to_all.10.in_ref = f32[16,16,8,128]{3,2,1,0:T(8,128)} all-to-all(f32[16,16,8,128]{3,2,1,0:T(8,128)S(1)} %bitcast.13), channel_id=1, replica_groups=mesh['dp'=16,'cls'=2] {'dp'}, dimensions={0} | all-to-all | bytes 2097152 | tf_op jit(solution)/shard_map/all_to_all | solution.py:171
  199.5 9.4 %shard_map.59 = f32[16,4,9,256]{3,2,1,0:T(8,128)} custom-call(f32[16,16,8,128]{3,2,1,0:T(8,128)} %all_to_all.10.in_ref), custom_call_target="tpu_custom_call" | custom-call | tf_op jit(solution)/shard_map/pallas_call | solution.py:172
  208.8 2.4 %copy.7 = f32[16,4,9,256]{3,1,2,0:T(4,128)} copy(f32[16,4,9,256]{3,2,1,0:T(8,128)} %shard_map.59) | data formatting | bytes 1179648 | tf_op jit(solution)/shard_map/pallas_call | solution.py:172
  (1 shorter events, 0.0 us)
Async XLA Ops:
  10.4 10.9 %copy-start.2 = (s32[2048]{0:T(1024)S(1)}, s32[2048]{0:T(1024)}, u32[]{:S(2)}) copy-start(s32[2048]{0:T(1024)} %param.6) | copy-start | bytes 24580
  10.4 11.5 %copy-start.1 = (f32[512,8]{0,1:T(8,128)S(1)}, f32[512,8]{0,1:T(8,128)}, u32[]{:S(2)}) copy-start(f32[512,8]{0,1:T(8,128)} %param.9) | copy-start | bytes 49156
  12.7 32.8 %all-to-all-start = ((bf16[16,16,2048]{2,1,0:T(8,128)(2,1)}), bf16[16,16,2048]{2,1,0:T(8,128)(2,1)S(1)}, u32[]{:S(2)}, u32[]{:S(2)}) async-start(bf16[16,16,2048]{2,1,0:T(8,128)(2,1)} %bitcast.12), calls=%async_computation | async-start | bytes 2097152 | tf_op jit(solution)/shard_map/all_to_all | solution.py:131
  21.1 75.4 %all-gather.4.cloned.1.call-start = ((), (), s32[]{:S(2)}) async-start(), calls=%async_computation.2 | async-start | bytes 1114112 | tf_op jit(solution)/shard_map/all_gather | solution.py:153
  96.4 1.2 copy-start
Sparse Core Ops, SparseCore 0:
  39.8 56.5 all-gather.3

commit v2 on v1

v2 whole, which is shorter than its diff:
```python
import functools

import jax
import jax.numpy as jnp
from jax import lax
from jax.experimental import pallas as pl
from jax.experimental.pallas import tpu as pltpu
from jax.sharding import PartitionSpec as P

BINS = 256
NODES = 4
STATS = 9
SLOT = 16
HIGH = lax.Precision.HIGHEST
MESH = pl.DeviceIdType.MESH
F8 = jnp.float8_e4m3fn
FIRST, SECOND, THIRD = 32.0, 16.0, float(2**22)
NT = (((1,), (1,)), ((), ()))


def codes_kernel(codes_ref, out_ref):
    out_ref[...] = codes_ref[...].astype(jnp.float32).T.astype(jnp.bfloat16)


def softmax_kernel(scores_ref, labels_ref, sketch_ref, out_ref):
    values = scores_ref[...].astype(jnp.float32)
    rows, classes = values.shape
    top = jnp.max(values, axis=1, keepdims=True)
    expo = jnp.exp(values - top)
    left = sketch_ref[...]
    sums = lax.dot_general(left, expo, NT, precision=HIGH, preferred_element_type=jnp.float32)
    squares = lax.dot_general(
        left[8:16], expo * expo, NT, precision=HIGH, preferred_element_type=jnp.float32
    )
    hit = lax.broadcasted_iota(jnp.int32, (classes, rows), 0) == labels_ref[...]
    picked = jnp.dot(
        left[0:8], hit.astype(jnp.float32), precision=HIGH, preferred_element_type=jnp.float32
    )
    tops = jnp.broadcast_to(top, (rows, 128)).T[0:1]
    out_ref[0:8] = sums[0:8]
    out_ref[8:16] = picked
    where = lax.broadcasted_iota(jnp.int32, (8, rows), 0)
    out_ref[16:24] = jnp.where(where == 0, tops, jnp.where(where == 1, sums[8:9], squares[0:1]))


def combine(parts_ref, nodes_ref):
    parts = parts_ref.shape[0]
    top = parts_ref[0, 16:17]
    for i in range(1, parts):
        top = jnp.maximum(top, parts_ref[i, 16:17])
    sketched = label = total = squares = 0.0
    for i in range(parts):
        scale = jnp.exp(parts_ref[i, 16:17] - top)
        sketched += parts_ref[i, 0:8] * scale
        label += parts_ref[i, 8:16]
        total += parts_ref[i, 17:18] * scale
        squares += parts_ref[i, 18:19] * (scale * scale)
    grad = sketched / total - label
    hessian = 1.0 - squares / (total * total)
    where = lax.broadcasted_iota(jnp.int32, grad.shape, 0)
    tail = jnp.where(where == 0, hessian, jnp.where(where == 1, nodes_ref[...].astype(jnp.float32), 0.0))
    return jnp.concatenate([grad, tail], axis=0).astype(jnp.bfloat16)


def split_weights(stats, left_ref):
    node = stats[STATS:STATS + 1]
    wide = stats.astype(jnp.float32) * FIRST
    wide = jnp.where(lax.broadcasted_iota(jnp.int32, wide.shape, 0) < STATS, wide, 0.0)
    first = wide.astype(F8).astype(jnp.float32)
    rest = wide - first
    second = (rest * SECOND).astype(F8).astype(jnp.float32)
    third = ((rest - second * (1.0 / SECOND)) * THIRD).astype(F8)
    zero = jnp.zeros((), jnp.bfloat16)
    span = NODES * SLOT
    masks = [node == jnp.full((), n, jnp.bfloat16) for n in range(NODES)]
    for k, piece in enumerate((first, second, third)):
        piece = piece.astype(jnp.bfloat16)
        rows = jnp.concatenate([jnp.where(mask, piece, zero) for mask in masks], axis=0).astype(F8)
        left_ref[k * span:(k + 1) * span] = rows
        if k == 2:
            left_ref[3 * span:4 * span] = rows


def main_kernel(
    dp, cls, pair, width, parts_ref, nodes_ref, codes_ref, out_ref,
    parts_buf, stats_buf, left_ref, acc_ref, send_buf, recv_buf,
    part_send, part_recv, stat_send, stat_recv, hist_send, hist_recv,
):
    me = lax.axis_index("dp")
    mine = lax.axis_index("cls")
    rows = nodes_ref.shape[1]
    own = codes_ref.shape[1]
    groups = own // pair
    bins = BINS // dp

    def part_copy(e):
        return pltpu.make_async_remote_copy(
            src_ref=parts_buf.at[0], dst_ref=parts_buf.at[e],
            send_sem=part_send.at[e], recv_sem=part_recv.at[e],
            device_id={"cls": lax.rem(mine + e, cls)}, device_id_type=MESH,
        )

    def stat_copy(d):
        return pltpu.make_async_remote_copy(
            src_ref=stats_buf.at[0], dst_ref=stats_buf.at[d],
            send_sem=stat_send.at[d], recv_sem=stat_recv.at[d],
            device_id={"dp": lax.rem(me + d, dp)}, device_id_type=MESH,
        )

    def hist_copy(d):
        to = lax.rem(me + d, dp)
        return pltpu.make_async_remote_copy(
            src_ref=send_buf.at[pl.ds(to * bins, bins)], dst_ref=recv_buf.at[me],
            send_sem=hist_send.at[d], recv_sem=hist_recv.at[d],
            device_id={"dp": to}, device_id_type=MESH,
        )

    barrier = pltpu.get_barrier_semaphore()

    @pl.loop(1, dp)
    def _(d):
        pl.semaphore_signal(barrier, inc=1, device_id={"dp": lax.rem(me + d, dp)}, device_id_type=MESH)

    @pl.loop(1, cls)
    def _(e):
        pl.semaphore_signal(barrier, inc=1, device_id={"cls": lax.rem(mine + e, cls)}, device_id_type=MESH)

    parts_buf[0] = parts_ref[...]
    pl.semaphore_wait(barrier, dp + cls - 2)

    @pl.loop(1, cls)
    def _(e):
        part_copy(e).start()

    acc_ref[...] = jnp.zeros_like(acc_ref)

    @pl.loop(1, cls)
    def _(e):
        part_copy(e).wait_recv()

    stats_buf[0] = combine(parts_buf, nodes_ref)

    @pl.loop(1, dp)
    def _(d):
        stat_copy(d).start()

    bin_ids = lax.broadcasted_iota(jnp.int32, (BINS, width), 0).astype(jnp.bfloat16)
    one = jnp.ones((), jnp.bfloat16)
    zero = jnp.zeros((), jnp.bfloat16)

    @pl.loop(0, dp)
    def _(d):
        @pl.when(d > 0)
        def _():
            stat_copy(d).wait_recv()

        split_weights(stats_buf[d], left_ref)
        source = lax.rem(me - d + dp, dp)
        for f in range(own):
            total = None
            for c in range(rows // width):
                cut = slice(c * width, (c + 1) * width)
                code = codes_ref[source, f:f + 1, cut]
                hit = jnp.where(code == bin_ids, one, zero).astype(F8)
                term = lax.dot_general(hit, left_ref[:, cut], NT, preferred_element_type=jnp.float32)
                total = term if total is None else total + term
            acc_ref[f] += total

    span = NODES * SLOT
    lane = lax.broadcasted_iota(jnp.int32, (BINS, 2 * span), 1)
    scale = jnp.where(lane < span, 1.0 / FIRST, 1.0 / (FIRST * SECOND))

    def whole(f):
        low = acc_ref[f, :, 0:2 * span] * scale
        high = acc_ref[f, :, 2 * span:4 * span] * (1.0 / (FIRST * THIRD))
        return low + pltpu.roll(low, span, 1) + high

    for g in range(groups):
        value = whole(g)
        if pair == 2:
            value = jnp.where(lane < span, value, whole(groups + g))
        send_buf[:, g, :] = value

    @pl.loop(1, dp)
    def _(d):
        hist_copy(d).start()

    recv_buf[me] = send_buf[pl.ds(me * bins, bins)]

    @pl.loop(1, dp)
    def _(d):
        hist_copy(d).wait_recv()

    width_out = dp * groups

    @pl.loop(0, bins)
    def _(b):
        block = recv_buf[:, b].reshape(width_out, 2 * span).T
        for i in range(pair):
            for n in range(NODES):
                at = (i * NODES + n) * SLOT
                out_ref[b, n, :, i * width_out:(i + 1) * width_out] = block[at:at + STATS]

    @pl.loop(1, cls)
    def _(e):
        part_copy(e).wait_send()

    @pl.loop(1, dp)
    def _(d):
        stat_copy(d).wait_send()
        hist_copy(d).wait_send()


def body(dp, cls, scores, labels, node_ids, codes, sketch):
    rows, classes = scores.shape
    feats = codes.shape[1]
    own = feats // dp
    pair = 2 if own % 2 == 0 else 1
    groups = own // pair
    block = min(512, rows)

    codes_t = pl.pallas_call(
        codes_kernel,
        grid=(rows // block,),
        in_specs=[pl.BlockSpec((block, feats), lambda i: (i, 0))],
        out_specs=pl.BlockSpec((feats, block), lambda i: (0, i)),
        out_shape=jax.ShapeDtypeStruct((feats, rows), jnp.bfloat16),
    )(codes)
    codes_t = codes_t.reshape(pair, dp, groups, rows).transpose(1, 0, 2, 3).reshape(dp, own, rows)
    codes_all = lax.all_to_all(codes_t, "dp", 0, 0, tiled=True)

    local = (labels - lax.axis_index("cls") * classes)[None, :]
    left = jnp.concatenate(
        [sketch.T, jnp.ones((1, classes), jnp.float32), jnp.zeros((7, classes), jnp.float32)], axis=0
    )
    parts = pl.pallas_call(
        softmax_kernel,
        grid=(rows // block,),
        in_specs=[
            pl.BlockSpec((block, classes), lambda i: (i, 0)),
            pl.BlockSpec((1, block), lambda i: (0, i)),
            pl.BlockSpec((16, classes), lambda i: (0, 0)),
        ],
        out_specs=pl.BlockSpec((24, block), lambda i: (0, i)),
        out_shape=jax.ShapeDtypeStruct((24, rows), jnp.float32),
    )(scores, local, left)
    bins = BINS // dp
    vmem = pl.BlockSpec(memory_space=pltpu.VMEM)
    return pl.pallas_call(
        functools.partial(main_kernel, dp, cls, pair, min(WIDTH, rows)),
        in_specs=[vmem] * 3,
        out_specs=vmem,
        out_shape=jax.ShapeDtypeStruct((bins, NODES, STATS, feats), jnp.float32),
        scratch_shapes=[
            pltpu.VMEM((cls, 24, rows), jnp.float32),
            pltpu.VMEM((dp, SLOT, rows), jnp.bfloat16),
            pltpu.VMEM((4 * NODES * SLOT, rows), F8),
            pltpu.VMEM((own, BINS, 4 * NODES * SLOT), jnp.float32),
            pltpu.VMEM((BINS, groups, 128), jnp.float32),
            pltpu.VMEM((dp, bins, groups, 128), jnp.float32),
            pltpu.SemaphoreType.DMA((cls,)),
            pltpu.SemaphoreType.DMA((cls,)),
            pltpu.SemaphoreType.DMA((dp,)),
            pltpu.SemaphoreType.DMA((dp,)),
            pltpu.SemaphoreType.DMA((dp,)),
            pltpu.SemaphoreType.DMA((dp,)),
        ],
        compiler_params=pltpu.CompilerParams(
            vmem_limit_bytes=50 << 20, collective_id=0, has_side_effects=True
        ),
    )(parts, node_ids[None, :], codes_all)


WIDTH = 512


def solution(mesh):
    return jax.shard_map(
        functools.partial(body, mesh.shape["dp"], mesh.shape["cls"]),
        mesh=mesh,
        in_specs=(P("dp", "cls"), P("dp"), P("dp"), P("dp", "cls"), P("cls", None)),
        out_specs=P("dp", None, None, "cls"),
        check_vma=False,
    )
```

time: 219 us -> 115 us (0.53)
  the two profiles are of different devices: /device:TPU:0 before, /device:TPU:15 now
where the time goes in v2:
time: 115 us; the launch traced here: 114 us
  Pallas kernels  90.9 us (79%)
  waiting for transfers between devices  10.7 us (9%)
  starting transfers between devices  6.71 us (6%)
  local copies, waits for them, and re-layouts  4.64 us (4%)
  other arithmetic  1.27 us (1%)
    pallas_call x1, Pallas kernels, body(): pl.pallas_call(functools.partial(main_kernel, dp, cls, pair, min(WIDTH, r...  75.3 us
    pallas_call x1, Pallas kernels, body(): pl.pallas_call(softmax_kernel, grid=(rows // block,), in_specs=[pl.BlockS...  11.8 us
    all_to_all x1, waiting for transfers between devices, body(): codes_all = lax.all_to_all(codes_t, 'dp', 0, 0, tiled=True)  10.7 us
    all_to_all x1, starting transfers between devices, body(): codes_all = lax.all_to_all(codes_t, 'dp', 0, 0, tiled=True)  6.71 us
    pallas_call x1, Pallas kernels, body(): pl.pallas_call(codes_kernel, grid=(rows // block,), in_specs=[pl.BlockSpe...  3.89 us
    reshape x1, local copies, waits for them, and re-layouts, body(): codes_t.reshape(pair, dp, groups, rows).transpose(1, 0, 2, 3)  2.33 us
  transfers between devices with their start and end apart: 1, of which 1 were waited for; matrix products, arithmetic and copies ran while one was open for 1% of the time, Pallas kernels for 10%

profile of v2, /device:TPU:15, one launch (start us, length us, event | category | flops | bytes accessed | tf_op | source)
XLA Modules:
  0.0 114.3 jit_solution(6285817375625215625)
XLA Ops:
  0.0 3.9 %shard_map.56 = bf16[256,2048]{1,0:T(8,128)(2,1)} custom-call(s32[2048,256]{1,0:T(8,128)} %codes_ref.1), custom_call_target="tpu_custom_call" | custom-call | tf_op jit(solution)/shard_map/pallas_call | solution.py:222
  3.9 0.0 copy-start.3
  3.9 0.0 copy-start.2
  3.9 2.3 %copy.9 = bf16[2,16,8,2048]{3,2,0,1:T(8,128)(2,1)} copy(bf16[2,16,8,2048]{3,2,1,0:T(8,128)(2,1)} %bitcast.11) | data formatting | bytes 2097152 | tf_op jit(solution)/shard_map/reshape | solution.py:229
  6.2 0.0 copy-start.1
  6.2 6.7 %all-to-all-start = ((bf16[16,16,2048]{2,1,0:T(8,128)(2,1)}), bf16[16,16,2048]{2,1,0:T(8,128)(2,1)S(1)}, u32[]{:S(2)}, u32[]{:S(2)}) async-start(bf16[16,16,2048]{2,1,0:T(8,128)(2,1)} %bitcast.9), calls=%async_computation | async-start | bytes 2097152 | tf_op jit(solution)/shard_map/all_to_all | solution.py:230
  12.9 0.1 pad.2.clone
  13.0 0.1 pad.1.clone
  13.1 0.0 copy-done.3
  13.1 0.6 broadcast_subtract_fusion
  13.7 0.0 copy-done.2
  13.7 0.7 maximum_maximum_fusion.sketch_ref
  14.4 11.8 %shard_map.55.parts_ref = f32[24,2048]{1,0:T(8,128)} custom-call(bf16[2048,512]{1,0:T(8,128)(2,1)} %scores_ref.1, s32[1,2048]{1,0:T(1,128)} %bitcast.12, f32[16,512]{1,0:T(8,128)} %maximum_maximum_fusion.sketch_ref), custom_call_target="tpu_custom_call" | custom-call | tf_op jit(solution)/shard_map/pallas_call | solution.py:236
  26.1 10.7 %all-to-all-done.codes_ref = bf16[16,16,2048]{2,1,0:T(8,128)(2,1)S(1)} async-done(((bf16[16,16,2048]{2,1,0:T(8,128)(2,1)}), bf16[16,16,2048]{2,1,0:T(8,128)(2,1)S(1)}, u32[]{:S(2)}, u32[]{:S(2)}) %all-to-all-start) | async-done | bytes 1048608 | tf_op jit(solution)/shard_map/all_to_all | solution.py:230
  36.9 0.0 copy-done.1
  36.9 0.0 copy-start
  36.9 0.9 copy-done
  37.8 75.3 %shard_map.57 = f32[16,4,9,256]{3,2,1,0:T(8,128)S(1)} custom-call(f32[24,2048]{1,0:T(8,128)S(1)} %copy-done, s32[1,2048]{1,0:T(1,128)S(1)} %bitcast.10, bf16[16,16,2048]{2,1,0:T(8,128)(2,1)S(1)} %all-to-all-done.codes_ref), custom_call_target="tpu_custom_call" | custom-call | tf_op jit(solution)/shard_map/pallas_call | solution.py:249
  113.1 1.2 %copy.7 = f32[16,4,9,256]{3,1,2,0:T(4,128)} copy(f32[16,4,9,256]{3,2,1,0:T(8,128)S(1)} %shard_map.57) | data formatting | bytes 1179648 | tf_op jit(solution)/shard_map/pallas_call | solution.py:249
  (1 shorter events, 0.0 us)
Async XLA Ops:
  3.9 9.2 %copy-start.3 = (s32[2048]{0:T(1024)S(1)}, s32[2048]{0:T(1024)}, u32[]{:S(2)}) copy-start(s32[2048]{0:T(1024)} %param.6) | copy-start | bytes 24580
  3.9 9.8 %copy-start.2 = (f32[512,8]{0,1:T(8,128)S(1)}, f32[512,8]{0,1:T(8,128)}, u32[]{:S(2)}) copy-start(f32[512,8]{0,1:T(8,128)} %param.9) | copy-start | bytes 49156
  6.2 30.6 %copy-start.1 = (s32[2048]{0:T(1024)S(1)}, s32[2048]{0:T(1024)}, u32[]{:S(2)}) copy-start(s32[2048]{0:T(1024)} %param.7) | copy-start | bytes 24580
  6.2 30.6 %all-to-all-start = ((bf16[16,16,2048]{2,1,0:T(8,128)(2,1)}), bf16[16,16,2048]{2,1,0:T(8,128)(2,1)S(1)}, u32[]{:S(2)}, u32[]{:S(2)}) async-start(bf16[16,16,2048]{2,1,0:T(8,128)(2,1)} %bitcast.9), calls=%async_computation | async-start | bytes 2097152 | tf_op jit(solution)/shard_map/all_to_all | solution.py:230
  36.9 0.9 copy-start

commit v3 on v2

--- a/solution.py
+++ b/solution.py
@@ -11,36 +11,60 @@
 NODES = 4
 STATS = 9
 SLOT = 16
-HIGH = lax.Precision.HIGHEST
 MESH = pl.DeviceIdType.MESH
 F8 = jnp.float8_e4m3fn
 FIRST, SECOND, THIRD = 32.0, 16.0, float(2**22)
 NT = (((1,), (1,)), ((), ()))
 
 
-def codes_kernel(codes_ref, out_ref):
-    out_ref[...] = codes_ref[...].astype(jnp.float32).T.astype(jnp.bfloat16)
-
-
-def softmax_kernel(scores_ref, labels_ref, sketch_ref, out_ref):
-    values = scores_ref[...].astype(jnp.float32)
-    rows, classes = values.shape
-    top = jnp.max(values, axis=1, keepdims=True)
-    expo = jnp.exp(values - top)
-    left = sketch_ref[...]
-    sums = lax.dot_general(left, expo, NT, precision=HIGH, preferred_element_type=jnp.float32)
-    squares = lax.dot_general(
-        left[8:16], expo * expo, NT, precision=HIGH, preferred_element_type=jnp.float32
-    )
-    hit = lax.broadcasted_iota(jnp.int32, (classes, rows), 0) == labels_ref[...]
-    picked = jnp.dot(
-        left[0:8], hit.astype(jnp.float32), precision=HIGH, preferred_element_type=jnp.float32
-    )
-    tops = jnp.broadcast_to(top, (rows, 128)).T[0:1]
-    out_ref[0:8] = sums[0:8]
-    out_ref[8:16] = picked
-    where = lax.broadcasted_iota(jnp.int32, (8, rows), 0)
-    out_ref[16:24] = jnp.where(where == 0, tops, jnp.where(where == 1, sums[8:9], squares[0:1]))
+def turn_codes(codes_ref, codes_send, pair, block):
+    rows, feats = codes_ref.shape
+    dp, own, _ = codes_send.shape
+    groups = own // pair
+
+    @pl.loop(0, rows // block)
+    def _(i):
+        at = pl.ds(pl.multiple_of(i * block, block), block)
+        turned = codes_ref[at].astype(jnp.float32).T
+        for k in range(dp):
+            picked = [turned[(j * dp + k) * groups:(j * dp + k + 1) * groups] for j in range(pair)]
+            picked = picked[0] if pair == 1 else jnp.concatenate(picked, axis=0)
+            codes_send[k, :, at] = picked.astype(jnp.bfloat16)
+
+
+def class_sums(scores_ref, labels_ref, sketch_ref, parts_buf, first_class, block):
+    rows, classes = scores_ref.shape
+    sketch = sketch_ref[...]
+    high = sketch.astype(jnp.bfloat16)
+    rest = sketch - high.astype(jnp.float32)
+    mid = rest.astype(jnp.bfloat16)
+    low = rest - mid.astype(jnp.float32)
+    left = jnp.concatenate(
+        [high.astype(jnp.float32), mid.astype(jnp.float32), low, jnp.zeros_like(low)], axis=0
+    ).astype(jnp.bfloat16)
+    one = jnp.ones((), jnp.float32)
+    zero = jnp.zeros((), jnp.float32)
+    class_ids = lax.broadcasted_iota(jnp.int32, (classes, block), 0)
+    where = lax.broadcasted_iota(jnp.int32, (8, block), 0)
+
+    def times(right):
+        out = jnp.dot(left, right, preferred_element_type=jnp.float32)
+        return out[0:8] + out[8:16] + out[16:24]
+
+    @pl.loop(0, rows // block)
+    def _(i):
+        at = pl.ds(pl.multiple_of(i * block, block), block)
+        values = scores_ref[at].astype(jnp.float32).T
+        top = jnp.max(values, axis=0, keepdims=True)
+        expo = jnp.exp(values - top)
+        total = jnp.sum(expo, axis=0, keepdims=True)
+        squares = jnp.sum(expo * expo, axis=0, keepdims=True)
+        coarse = expo.astype(jnp.bfloat16)
+        fine = (expo - coarse.astype(jnp.float32)).astype(jnp.bfloat16)
+        hit = jnp.where(class_ids == labels_ref[:, at] - first_class, one, zero).astype(jnp.bfloat16)
+        parts_buf[0, 0:8, at] = times(coarse) + times(fine)
+        parts_buf[0, 8:16, at] = times(hit)
+        parts_buf[0, 16:24, at] = jnp.where(where == 0, top, jnp.where(where == 1, total, squares))
 
 
 def combine(parts_ref, nodes_ref):
@@ -82,16 +106,24 @@
 
 
 def main_kernel(
-    dp, cls, pair, width, parts_ref, nodes_ref, codes_ref, out_ref,
-    parts_buf, stats_buf, left_ref, acc_ref, send_buf, recv_buf,
-    part_send, part_recv, stat_send, stat_recv, hist_send, hist_recv,
+    dp, cls, pair, width, scores_ref, labels_ref, nodes_ref, codes_ref, sketch_ref, out_ref,
+    codes_send, codes_buf, parts_buf, stats_buf, left_ref, acc_ref, send_buf, recv_buf,
+    code_send, code_recv, part_send, part_recv, stat_send, stat_recv, hist_send, hist_recv,
 ):
     me = lax.axis_index("dp")
     mine = lax.axis_index("cls")
     rows = nodes_ref.shape[1]
-    own = codes_ref.shape[1]
+    own = codes_buf.shape[1]
     groups = own // pair
     bins = BINS // dp
+
+    def code_copy(d):
+        to = lax.rem(me + d, dp)
+        return pltpu.make_async_remote_copy(
+            src_ref=codes_send.at[to], dst_ref=codes_buf.at[d],
+            send_sem=code_send.at[d], recv_sem=code_recv.at[d],
+            device_id={"dp": to}, device_id_type=MESH,
+        )
 
     def part_copy(e):
         return pltpu.make_async_remote_copy(
@@ -125,8 +157,17 @@
     def _(e):
         pl.semaphore_signal(barrier, inc=1, device_id={"cls": lax.rem(mine + e, cls)}, device_id_type=MESH)
 
-    parts_buf[0] = parts_ref[...]
+    turn_codes(codes_ref, codes_send, pair, min(BLOCK, rows))
     pl.semaphore_wait(barrier, dp + cls - 2)
+
+    @pl.loop(1, dp)
+    def _(d):
+        code_copy(d).start()
+
+    codes_buf[0] = codes_send[me]
+    class_sums(
+        scores_ref, labels_ref, sketch_ref, parts_buf, mine * scores_ref.shape[1], min(BLOCK, rows)
+    )
 
     @pl.loop(1, cls)
     def _(e):
@@ -152,15 +193,15 @@
     def _(d):
         @pl.when(d > 0)
         def _():
+            code_copy(d).wait_recv()
             stat_copy(d).wait_recv()
 
         split_weights(stats_buf[d], left_ref)
-        source = lax.rem(me - d + dp, dp)
         for f in range(own):
             total = None
             for c in range(rows // width):
                 cut = slice(c * width, (c + 1) * width)
-                code = codes_ref[source, f:f + 1, cut]
+                code = codes_buf[d, f:f + 1, cut]
                 hit = jnp.where(code == bin_ids, one, zero).astype(F8)
                 term = lax.dot_general(hit, left_ref[:, cut], NT, preferred_element_type=jnp.float32)
                 total = term if total is None else total + term
@@ -207,57 +248,35 @@
 
     @pl.loop(1, dp)
     def _(d):
+        code_copy(d).wait_send()
         stat_copy(d).wait_send()
         hist_copy(d).wait_send()
 
 
 def body(dp, cls, scores, labels, node_ids, codes, sketch):
-    rows, classes = scores.shape
+    rows = scores.shape[0]
     feats = codes.shape[1]
     own = feats // dp
     pair = 2 if own % 2 == 0 else 1
     groups = own // pair
-    block = min(512, rows)
-
-    codes_t = pl.pallas_call(
-        codes_kernel,
-        grid=(rows // block,),
-        in_specs=[pl.BlockSpec((block, feats), lambda i: (i, 0))],
-        out_specs=pl.BlockSpec((feats, block), lambda i: (0, i)),
-        out_shape=jax.ShapeDtypeStruct((feats, rows), jnp.bfloat16),
-    )(codes)
-    codes_t = codes_t.reshape(pair, dp, groups, rows).transpose(1, 0, 2, 3).reshape(dp, own, rows)
-    codes_all = lax.all_to_all(codes_t, "dp", 0, 0, tiled=True)
-
-    local = (labels - lax.axis_index("cls") * classes)[None, :]
-    left = jnp.concatenate(
-        [sketch.T, jnp.ones((1, classes), jnp.float32), jnp.zeros((7, classes), jnp.float32)], axis=0
-    )
-    parts = pl.pallas_call(
-        softmax_kernel,
-        grid=(rows // block,),
-        in_specs=[
-            pl.BlockSpec((block, classes), lambda i: (i, 0)),
-            pl.BlockSpec((1, block), lambda i: (0, i)),
-            pl.BlockSpec((16, classes), lambda i: (0, 0)),
-        ],
-        out_specs=pl.BlockSpec((24, block), lambda i: (0, i)),
-        out_shape=jax.ShapeDtypeStruct((24, rows), jnp.float32),
-    )(scores, local, left)
     bins = BINS // dp
     vmem = pl.BlockSpec(memory_space=pltpu.VMEM)
     return pl.pallas_call(
         functools.partial(main_kernel, dp, cls, pair, min(WIDTH, rows)),
-        in_specs=[vmem] * 3,
+        in_specs=[vmem] * 5,
         out_specs=vmem,
         out_shape=jax.ShapeDtypeStruct((bins, NODES, STATS, feats), jnp.float32),
         scratch_shapes=[
+            pltpu.VMEM((dp, own, rows), jnp.bfloat16),
+            pltpu.VMEM((dp, own, rows), jnp.bfloat16),
             pltpu.VMEM((cls, 24, rows), jnp.float32),
             pltpu.VMEM((dp, SLOT, rows), jnp.bfloat16),
             pltpu.VMEM((4 * NODES * SLOT, rows), F8),
             pltpu.VMEM((own, BINS, 4 * NODES * SLOT), jnp.float32),
             pltpu.VMEM((BINS, groups, 128), jnp.float32),
             pltpu.VMEM((dp, bins, groups, 128), jnp.float32),
+            pltpu.SemaphoreType.DMA((dp,)),
+            pltpu.SemaphoreType.DMA((dp,)),
             pltpu.SemaphoreType.DMA((cls,)),
             pltpu.SemaphoreType.DMA((cls,)),
             pltpu.SemaphoreType.DMA((dp,)),
@@ -268,10 +287,11 @@
         compiler_params=pltpu.CompilerParams(
             vmem_limit_bytes=50 << 20, collective_id=0, has_side_effects=True
         ),
-    )(parts, node_ids[None, :], codes_all)
+    )(scores, labels[None, :], node_ids[None, :], codes, sketch.T)
 
 
 WIDTH = 512
+BLOCK = 256
 
 
 def solution(mesh):

time: 115 us -> 106 us (0.922)
  waiting for transfers between devices: 10.7 us -> 0 us
  Pallas kernels: 90.9 us -> 101 us
  starting transfers between devices: 6.71 us -> 0 us
  other arithmetic: 1.27 us -> 0 us
    pallas_call x1, Pallas kernels: 75.3 us -> 101 us  [body(): pl.pallas_call(functools.partial(main_kernel, dp, cls, pair, min(WIDTH, r...]
    pallas_call x2 -> x0, Pallas kernels: 15.7 us -> none  [the longest x1 11.8 us: body(): pl.pallas_call(softmax_kernel, grid=(rows // block,), in_specs=[pl.BlockS...]
    all_to_all x1 -> x0, waiting for transfers between devices: 10.7 us -> none  [body(): codes_all = lax.all_to_all(codes_t, 'dp', 0, 0, tiled=True)]
    all_to_all x1 -> x0, starting transfers between devices: 6.71 us -> none  [body(): codes_all = lax.all_to_all(codes_t, 'dp', 0, 0, tiled=True)]
    unnamed x8, local copies, waits for them, and re-layouts: 0.94 us -> 3.7 us
    reshape x1 -> x0, local copies, waits for them, and re-layouts: 2.33 us -> none  [body(): codes_t.reshape(pair, dp, groups, rows).transpose(1, 0, 2, 3)]
  transfers between devices with their start and end apart: 1 -> 0, of which waited for: 1 -> 0; matrix products, arithmetic and copies ran while one was open for 1% -> 0% of each run, Pallas kernels for 10% -> 0%
where the time goes in v3:
time: 106 us
  Pallas kernels  101 us (95%)
  local copies, waits for them, and re-layouts  4.92 us (5%)
    pallas_call x1, Pallas kernels, body(): pl.pallas_call(functools.partial(main_kernel, dp, cls, pair, min(WIDTH, r...  101 us
    unnamed x8, local copies, waits for them, and re-layouts  3.7 us

profile of v3, /device:TPU:15, one launch (start us, length us, event | category | flops | bytes accessed | tf_op | source)
XLA Modules:
  0.0 105.6 jit_solution(11550015098996070904)
XLA Ops:
  0.0 0.0 copy-start
  0.0 1.6 %copy-done = bf16[2048,512]{1,0:T(8,128)(2,1)S(1)} copy-done((bf16[2048,512]{1,0:T(8,128)(2,1)S(1)}, bf16[2048,512]{1,0:T(8,128)(2,1)}, u32[]{:S(2)}) %copy-start) | copy-done | bytes 2097176
  1.6 0.0 copy-start.1
  1.6 0.7 copy-done.1
  2.3 0.0 copy-start.2
  2.3 0.7 copy-done.2
  3.0 0.0 copy-start.3
  3.0 0.7 copy-done.3
  3.7 100.7 %shard_map.55 = f32[16,4,9,256]{3,2,1,0:T(8,128)S(1)} custom-call(bf16[2048,512]{1,0:T(8,128)(2,1)S(1)} %copy-done, s32[1,2048]{1,0:T(1,128)S(1)} %bitcast.4, s32[1,2048]{1,0:T(1,128)S(1)} %bitcast.5, s32[2048,256]{1,0:T(8,128)} %codes_ref.1, f32[8,512]{1,0:T(8,128)S(1)} %bitcast.3), custom_call_target="tpu_custom_call" | custom-call | tf_op jit(solution)/shard_map/pallas_call | solution.py:264
  104.4 1.2 %copy.6 = f32[16,4,9,256]{3,1,2,0:T(4,128)} copy(f32[16,4,9,256]{3,2,1,0:T(8,128)S(1)} %shard_map.55) | data formatting | bytes 1179648 | tf_op jit(solution)/shard_map/pallas_call | solution.py:264
Async XLA Ops:
  0.0 1.6 %copy-start = (bf16[2048,512]{1,0:T(8,128)(2,1)S(1)}, bf16[2048,512]{1,0:T(8,128)(2,1)}, u32[]{:S(2)}) copy-start(bf16[2048,512]{1,0:T(8,128)(2,1)} %scores_ref.1) | copy-start | bytes 6291460
  1.6 0.7 copy-start.1
  2.3 0.7 copy-start.2
  3.0 0.7 copy-start.3
